TPU v7x, 128 devices: a whole 4x4x4 slice. The times are simulated.
128 devices in a mesh: row: 32 (over y, z, core), col: 4 (over x).
Axes of the slice: x: 4, y: 4, z: 4, core: 2. Of those that a mesh axis runs over, the one named last changes fastest.
Arguments:
- tile_values: bfloat16 [5632, 4, 256, 256], P('row', 'col'), may hold values from -0.375 to 0.375
- tile_rows: int32 [5632, 4], P('row', 'col'), may hold values from 0 to 15, as said below
- tile_source: int32 [5632, 4], P('row', 'col'), may hold values from 0 to 31
- tile_slot: int32 [5632, 4], P('row', 'col'), may hold values from 0 to 1
- send_lists: int32 [32, 4, 32, 2], P('row', 'col'), may hold values from 0 to 7
- basis_blocks: bfloat16 [256, 4, 256, 256], P('row', 'col'), may hold values from -6 to 6
Outputs:
- new_basis: float32 [131072, 256], P(('row', 'col'))
- triangle: float32 [256, 256], replicated
Inputs may be any that keep to these rules, and one draw needn't show every extreme that they name: `tile_rows`: in every slab and group each of the 16 block rows holds at least one tile.
All inputs are finite; a program needn't handle non-finite values.
Results may differ from a plain program's by a relative error of at most 0.0015.
Values may be sent and summed in bfloat16 or wider, within the bound.
No kernel may reach another device: no remote copies, remote signals or barrier semaphores. Data moves between devices by JAX's collectives and lax.ppermute only.
A program may use at most 256 MiB of HBM per device.

v0:
```python
import jax
import jax.numpy as jnp
from jax import lax
from jax.sharding import PartitionSpec as P

BR_DEV = 16


def upper_factor(gram):
    width = gram.shape[0]
    index = jnp.arange(width, dtype=jnp.int32)

    def row_fill(j, upper):
        unit = (index == j).astype(jnp.float32)
        known = jnp.dot(upper, unit, precision=lax.Precision.HIGHEST)
        target = lax.dynamic_index_in_dim(gram, j, 0, keepdims=False)
        residue = target - jnp.dot(known, upper, precision=lax.Precision.HIGHEST)
        pivot = jnp.sqrt(lax.dynamic_index_in_dim(residue, j, 0, keepdims=False))
        filled = jnp.where(index >= j, residue / pivot, jnp.float32(0.0))
        return upper + unit[:, None] * filled[None, :]

    return lax.fori_loop(0, width, row_fill, jnp.zeros((width, width), jnp.float32))


def upper_inverse(upper):
    width = upper.shape[0]
    index = jnp.arange(width, dtype=jnp.int32)

    def row_step(step, inverse):
        i = (width - 1 - step).astype(jnp.int32)
        row_now = lax.dynamic_index_in_dim(upper, i, 0, keepdims=False)
        pivot = lax.dynamic_index_in_dim(row_now, i, 0, keepdims=False)
        unit = (index == i).astype(jnp.float32)
        solved = (unit - jnp.dot(row_now, inverse, precision=lax.Precision.HIGHEST)) / pivot
        return jnp.where((index == i)[:, None], solved[None, :], inverse)

    return lax.fori_loop(0, width, row_step, jnp.zeros((width, width), jnp.float32))


def local(tile_values, tile_rows, tile_source, tile_slot, send_lists, basis_blocks):
    values = tile_values[:, 0]
    blocks_row = tile_rows[:, 0]
    source = tile_source[:, 0]
    slotted = tile_slot[:, 0]
    owned = basis_blocks[:, 0]
    slot_count = send_lists.shape[3]
    rank_width = owned.shape[2]
    outgoing = owned[send_lists[0, 0]]
    arrived = lax.all_to_all(outgoing, "row", split_axis=0, concat_axis=0, tiled=True)
    flatten = arrived.reshape(-1, arrived.shape[2], arrived.shape[3])
    chosen = flatten[source * slot_count + slotted]
    product = jnp.einsum("tij,tjk->tik", values, chosen, preferred_element_type=jnp.float32)
    selector = (blocks_row[None, :] == jnp.arange(BR_DEV, dtype=jnp.int32)[:, None]).astype(
        jnp.float32
    )
    partial_value = jnp.einsum("bt,tik->bik", selector, product, precision=lax.Precision.HIGHEST)
    partial_value = partial_value.reshape(-1, rank_width)
    local_y = lax.psum_scatter(partial_value, "col", scatter_dimension=0, tiled=True)
    gram = jnp.dot(local_y.T, local_y, precision=lax.Precision.HIGHEST)
    summed = lax.psum(gram, ("row", "col"))
    upper = upper_factor(summed)
    cells_all = local_y.shape[0] * lax.axis_size("row") * lax.axis_size("col")
    scale = jnp.sqrt(jnp.float32(cells_all))
    solved = jnp.dot(local_y, upper_inverse(upper), precision=lax.Precision.HIGHEST)
    return (solved * scale, upper / scale)


def solution(mesh):
    return jax.shard_map(
        local,
        mesh=mesh,
        in_specs=(
            P("row", "col", None, None),
            P("row", "col"),
            P("row", "col"),
            P("row", "col"),
            P("row", "col", None, None),
            P("row", "col", None, None),
        ),
        out_specs=(P(("row", "col"), None), P()),
        check_vma=False,
    )
```

profile of v0, /device:TPU:1, one launch (start us, length us, event | category | flops | bytes accessed | tf_op | source)
XLA Modules:
  0.0 1576.3 jit_solution(10319401639767442812)
XLA Ops:
  7.2 0.8 compare_select_fusion.2
  8.4 5.5 gather_fusion
  13.9 9.6 all-to-all-start
  23.7 108.4 %all-to-all-done = bf16[32,2,256,256]{3,2,1,0:T(8,128)(2,1)} async-done(((bf16[32,2,256,256]{3,2,1,0:T(8,128)(2,1)}), bf16[32,2,256,256]{3,2,1,0:T(8,128)(2,1)}, u32[]{:S(2)}, u32[]{:S(2)}) %all-to-all-start) | async-done | bytes 8388640 | tf_op jit(solution)/shard_map/all_to_all | solution.py:49
  132.1 13.8 gather_fusion.1
  145.9 37.6 %fusion.24 = f32[176,256,256]{2,1,0:T(8,128)} fusion(bf16[176,256,256]{2,1,0:T(8,128)(2,1)} %gather_fusion.1, bf16[176,1,256,256]{3,2,1,0:T(8,128)(2,1)} %param.10), kind=kOutput, calls=%fused_computation.32 | convolution fusion | flops 5905580032 | bytes 92274688 | tf_op jit(solution)/shard_map/tij,tjk->tik/dot_general | solution.py:52
  183.5 46.6 %copy.11 = f32[176,256,256]{1,0,2:T(8,128)} copy(f32[176,256,256]{2,1,0:T(8,128)} %fusion.24) | data formatting | bytes 92274688 | tf_op jit(solution)/shard_map/tij,tjk->tik/dot_general | solution.py:52
  230.1 20.4 %fusion.22 = f32[16,256,256]{2,0,1:T(8,128)S(1)} fusion(f32[176,256,256]{1,0,2:T(8,128)} %copy.11, s32[176]{0:T(256)S(1)} %bitcast.63), kind=kOutput, calls=%fused_computation.30 | convolution fusion | flops 2214595328 | bytes 50332352 | tf_op jit(solution)/shard_map/bt,tik->bik/dot_general | solution.py:56
  250.5 4.4 copy.10
  255.1 61.9 %reduce-scatter.2.cloned.1.call-done = f32[1024,256]{1,0:T(8,128)} async-done(((f32[4096,256]{1,0:T(8,128)}), f32[1024,256]{1,0:T(8,128)}) %reduce-scatter.2.cloned.1.call-update) | async-done | bytes 1048592 | tf_op jit(solution)/shard_map/reduce_scatter | solution.py:58
  317.0 4.1 fusion.29
  321.1 143.2 %all-reduce.2.cloned.1.call-done = f32[256,256]{1,0:T(8,128)} async-done(((f32[256,256]{1,0:T(8,128)}), f32[256,256]{1,0:T(8,128)}) %all-reduce.2.cloned.1.call-update) | async-done | bytes 262160 | tf_op jit(solution)/shard_map/psum | solution.py:60
  464.3 680.8 %while.33 = (s32[]{:T(128)}, f32[256,256]{1,0:T(8,128)S(1)}, f32[256,256]{1,0:T(8,128)}, s32[]{:T(128)}, s32[]{:T(128)}) while((s32[]{:T(128)}, f32[256,256]{1,0:T(8,128)S(1)}, f32[256,256]{1,0:T(8,128)}, s32[]{:T(128)}, s32[]{:T(128)}) %tuple.80), condition=%wide.region_3.4_spmd.clone.clone, body=%wide.region_2.3_spmd.clone.clone.sunk | while | flops 1902083 | bytes 1063021 | solution.py:22
  467.5 0.7 constant_dynamic-slice_fusion.2
  470.1 0.7 constant_dynamic-slice_fusion.2
  475.4 0.7 constant_dynamic-slice_fusion.2
  478.1 0.7 constant_dynamic-slice_fusion.2
  486.1 0.7 constant_dynamic-slice_fusion.2
  494.1 0.7 constant_dynamic-slice_fusion.2
  496.7 0.7 constant_dynamic-slice_fusion.2
  502.0 0.7 constant_dynamic-slice_fusion.2
  504.7 0.7 constant_dynamic-slice_fusion.2
  510.0 0.7 constant_dynamic-slice_fusion.2
  512.7 0.7 constant_dynamic-slice_fusion.2
  518.0 0.7 constant_dynamic-slice_fusion.2
  520.7 0.7 constant_dynamic-slice_fusion.2
  526.0 0.7 constant_dynamic-slice_fusion.2
  528.6 0.7 constant_dynamic-slice_fusion.2
  536.6 0.7 constant_dynamic-slice_fusion.2
  544.6 0.7 constant_dynamic-slice_fusion.2
  547.2 0.7 constant_dynamic-slice_fusion.2
  552.6 0.7 constant_dynamic-slice_fusion.2
  555.2 0.7 constant_dynamic-slice_fusion.2
  560.5 0.7 constant_dynamic-slice_fusion.2
  563.2 0.7 constant_dynamic-slice_fusion.2
  568.5 0.7 constant_dynamic-slice_fusion.2
  571.2 0.7 constant_dynamic-slice_fusion.2
  576.5 0.7 constant_dynamic-slice_fusion.2
  579.2 0.7 constant_dynamic-slice_fusion.2
  587.1 0.7 constant_dynamic-slice_fusion.2
  595.1 0.7 constant_dynamic-slice_fusion.2
  597.8 0.7 constant_dynamic-slice_fusion.2
  603.1 0.7 constant_dynamic-slice_fusion.2
  605.8 0.7 constant_dynamic-slice_fusion.2
  611.1 0.7 constant_dynamic-slice_fusion.2
  613.7 0.7 constant_dynamic-slice_fusion.2
  619.1 0.7 constant_dynamic-slice_fusion.2
  621.7 0.7 constant_dynamic-slice_fusion.2
  627.0 0.7 constant_dynamic-slice_fusion.2
  629.7 0.7 constant_dynamic-slice_fusion.2
  637.7 0.7 constant_dynamic-slice_fusion.2
  645.6 0.7 constant_dynamic-slice_fusion.2
  648.3 0.7 constant_dynamic-slice_fusion.2
  653.6 0.7 constant_dynamic-slice_fusion.2
  656.3 0.7 constant_dynamic-slice_fusion.2
  661.6 0.7 constant_dynamic-slice_fusion.2
  664.3 0.7 constant_dynamic-slice_fusion.2
  669.6 0.7 constant_dynamic-slice_fusion.2
  672.2 0.7 constant_dynamic-slice_fusion.2
  677.6 0.7 constant_dynamic-slice_fusion.2
  680.2 0.7 constant_dynamic-slice_fusion.2
  688.2 0.7 constant_dynamic-slice_fusion.2
  1145.9 420.4 %while.32 = (s32[]{:T(128)}, f32[256,256]{1,0:T(8,128)S(1)}, f32[256,256]{1,0:T(8,128)S(1)}, s32[]{:T(128)}, s32[]{:T(128)}, /*index=5*/s32[]{:T(128)}, s32[]{:T(128)}) while((s32[]{:T(128)}, f32[256,256]{1,0:T(8,128)S(1)}, f32[256,256]{1,0:T(8,128)S(1)}, s32[]{:T(128)}, s32[]{:T(128)}, /*index=5*/s32[]{:T(128)}, s32[]{:T(128)}) %tuple.83), condition=%wide.region_5.6_spmd.clone, body=%wide.region_4.5_spmd.clone.sunk | while | flops 984328 | bytes 792242 | solution.py:37
  1566.2 3.2 convolution_multiply_fusion
  (3557 shorter events, 864.7 us)
Async XLA Ops:
  7.2 1.2 copy-start
  7.2 16.4 %copy-start.4 = (s32[176,1]{0,1:T(1,128)S(1)}, s32[176,1]{0,1:T(1,128)}, u32[]{:S(2)}) copy-start(s32[176,1]{0,1:T(1,128)} %param.12) | copy-start | bytes 2116
  7.2 16.4 %copy-start.3 = (s32[176,1]{0,1:T(1,128)S(1)}, s32[176,1]{0,1:T(1,128)}, u32[]{:S(2)}) copy-start(s32[176,1]{0,1:T(1,128)} %param.13) | copy-start | bytes 2116
  13.9 118.2 %all-to-all-start = ((bf16[32,2,256,256]{3,2,1,0:T(8,128)(2,1)}), bf16[32,2,256,256]{3,2,1,0:T(8,128)(2,1)}, u32[]{:S(2)}, u32[]{:S(2)}) async-start(bf16[32,2,256,256]{3,2,1,0:T(8,128)(2,1)} %bitcast.57), calls=%async_computation | async-start | bytes 16777216 | tf_op jit(solution)/shard_map/all_to_all | solution.py:49
  23.6 293.4 %reduce-scatter.2.cloned.1.call-start = ((), (), s32[]{:S(2)}) async-start(), calls=%async_computation.2 | async-start | bytes 5242880 | tf_op jit(solution)/shard_map/reduce_scatter | solution.py:58
  183.5 46.6 %copy-start.2 = (s32[176,1]{0,1:T(1,128)S(1)}, s32[176,1]{0,1:T(1,128)}, u32[]{:S(2)}) copy-start(s32[176,1]{0,1:T(1,128)} %param.11) | copy-start | bytes 2116
  230.1 1339.3 %copy-start.1 = (bf16[8,1,256,256]{3,2,1,0:T(8,128)(2,1)S(1)}, bf16[8,1,256,256]{3,2,1,0:T(8,128)(2,1)}, u32[]{:S(2)}) copy-start(bf16[8,1,256,256]{3,2,1,0:T(8,128)(2,1)} %param.15) | copy-start | bytes 3145732
  254.9 209.4 %all-reduce.2.cloned.1.call-start = ((), (), s32[]{:S(2)}) async-start(), calls=%async_computation.3 | async-start | bytes 524288 | tf_op jit(solution)/shard_map/psum | solution.py:60
Sparse Core Ops, SparseCore 0:
  255.0 61.9 reduce-scatter.1
  323.0 141.2 all-reduce.1
where the time goes:
time: 1600 us; the launch traced here: 1580 us
  local copies, waits for them, and re-layouts  577 us (36%)
  waiting for transfers between devices  314 us (20%)
  matrix products  233 us (15%)
  other arithmetic  227 us (14%)
  loops' own time  202 us (13%)
    dynamic_slice x256, local copies, waits for them, and re-layouts, row_fill(): target = lax.dynamic_index_in_dim(gram, j, 0, keepdims=False)  190 us
    another operation x1, loops' own time, upper_factor(): lax.fori_loop(0, width, row_fill, jnp.zeros((width, width), jnp.float32))  189 us
    dynamic_slice x256, local copies, waits for them, and re-layouts, row_step(): pivot = lax.dynamic_index_in_dim(row_now, i, 0, keepdims=False)  164 us
    div x256, other arithmetic, row_step(): (unit - jnp.dot(row_now, inverse, precision=lax.Precision.HIGHEST)) / pivot  163 us
    dynamic_slice x256, local copies, waits for them, and re-layouts, row_fill(): pivot = jnp.sqrt(lax.dynamic_index_in_dim(residue, j, 0, keepdims=False))  150 us
    psum x1, waiting for transfers between devices, local(): summed = lax.psum(gram, ('row', 'col'))  143 us
    all_to_all x1, waiting for transfers between devices, local(): lax.all_to_all(outgoing, 'row', split_axis=0, concat_axis=0, tiled=True)  108 us
    reduce_scatter x1, waiting for transfers between devices, local(): lax.psum_scatter(partial_value, 'col', scatter_dimension=0, tiled=True)  61.9 us
  transfers between devices with their start and end apart: 3, of which 3 were waited for; matrix products, arithmetic and copies ran while one was open for 0% of the time, Pallas kernels for 0%

commit v1 on v0

--- a/solution.py
+++ b/solution.py
@@ -57,7 +57,8 @@
     partial_value = partial_value.reshape(-1, rank_width)
     local_y = lax.psum_scatter(partial_value, "col", scatter_dimension=0, tiled=True)
     gram = jnp.dot(local_y.T, local_y, precision=lax.Precision.HIGHEST)
-    summed = lax.psum(gram, ("row", "col"))
+    val2 = jax.lax.psum(gram, axis_name="row")
+    summed = jax.lax.psum(val2, axis_name="col")
     upper = upper_factor(summed)
     cells_all = local_y.shape[0] * lax.axis_size("row") * lax.axis_size("col")
     scale = jnp.sqrt(jnp.float32(cells_all))

time: 1600 us -> 1580 us (0.988)
  loops' own time: 202 us -> 182 us
    another operation x1, loops' own time: 189 us -> 170 us  [upper_factor(): lax.fori_loop(0, width, row_fill, jnp.zeros((width, width), jnp.float32))]
    psum x1 -> x2, waiting for transfers between devices: 143 us -> 143 us  [the longest x1 101 us: local(): val2 = jax.lax.psum(gram, axis_name='row')]
  transfers between devices with their start and end apart: 3 -> 4, of which waited for: 3 -> 4; matrix products, arithmetic and copies ran while one was open for 0% -> 0% of each run, Pallas kernels for 0% -> 0%
where the time goes in v1:
time: 1580 us; the launch traced here: 1560 us
  local copies, waits for them, and re-layouts  577 us (37%)
  waiting for transfers between devices  313 us (20%)
  matrix products  233 us (15%)
  other arithmetic  227 us (14%)
  loops' own time  182 us (12%)
    dynamic_slice x256, local copies, waits for them, and re-layouts, row_fill(): target = lax.dynamic_index_in_dim(gram, j, 0, keepdims=False)  190 us
    another operation x1, loops' own time, upper_factor(): lax.fori_loop(0, width, row_fill, jnp.zeros((width, width), jnp.float32))  170 us
    dynamic_slice x256, local copies, waits for them, and re-layouts, row_step(): pivot = lax.dynamic_index_in_dim(row_now, i, 0, keepdims=False)  164 us
    div x256, other arithmetic, row_step(): (unit - jnp.dot(row_now, inverse, precision=lax.Precision.HIGHEST)) / pivot  163 us
    dynamic_slice x256, local copies, waits for them, and re-layouts, row_fill(): pivot = jnp.sqrt(lax.dynamic_index_in_dim(residue, j, 0, keepdims=False))  151 us
    all_to_all x1, waiting for transfers between devices, local(): lax.all_to_all(outgoing, 'row', split_axis=0, concat_axis=0, tiled=True)  108 us
    psum x1, waiting for transfers between devices, local(): val2 = jax.lax.psum(gram, axis_name='row')  101 us
    reduce_scatter x1, waiting for transfers between devices, local(): lax.psum_scatter(partial_value, 'col', scatter_dimension=0, tiled=True)  61.9 us
  transfers between devices with their start and end apart: 4, of which 4 were waited for; matrix products, arithmetic and copies ran while one was open for 0% of the time, Pallas kernels for 0%

profile of v1, /device:TPU:1, one launch (start us, length us, event | category | flops | bytes accessed | tf_op | source)
XLA Modules:
  0.0 1556.8 jit_solution(825358364358055254)
XLA Ops:
  7.2 0.8 compare_select_fusion.2
  8.4 5.5 gather_fusion
  13.9 9.6 all-to-all-start
  23.7 108.4 %all-to-all-done = bf16[32,2,256,256]{3,2,1,0:T(8,128)(2,1)} async-done(((bf16[32,2,256,256]{3,2,1,0:T(8,128)(2,1)}), bf16[32,2,256,256]{3,2,1,0:T(8,128)(2,1)}, u32[]{:S(2)}, u32[]{:S(2)}) %all-to-all-start) | async-done | bytes 8388640 | tf_op jit(solution)/shard_map/all_to_all | solution.py:49
  132.1 13.8 gather_fusion.1
  145.9 37.6 %fusion.24 = f32[176,256,256]{2,1,0:T(8,128)} fusion(bf16[176,256,256]{2,1,0:T(8,128)(2,1)} %gather_fusion.1, bf16[176,1,256,256]{3,2,1,0:T(8,128)(2,1)} %param.10), kind=kOutput, calls=%fused_computation.32 | convolution fusion | flops 5905580032 | bytes 92274688 | tf_op jit(solution)/shard_map/tij,tjk->tik/dot_general | solution.py:52
  183.5 46.6 %copy.11 = f32[176,256,256]{1,0,2:T(8,128)} copy(f32[176,256,256]{2,1,0:T(8,128)} %fusion.24) | data formatting | bytes 92274688 | tf_op jit(solution)/shard_map/tij,tjk->tik/dot_general | solution.py:52
  230.1 20.4 %fusion.22 = f32[16,256,256]{2,0,1:T(8,128)S(1)} fusion(f32[176,256,256]{1,0,2:T(8,128)} %copy.11, s32[176]{0:T(256)S(1)} %bitcast.63), kind=kOutput, calls=%fused_computation.30 | convolution fusion | flops 2214595328 | bytes 50332352 | tf_op jit(solution)/shard_map/bt,tik->bik/dot_general | solution.py:56
  250.5 4.4 copy.10
  255.1 61.9 %reduce-scatter.2.cloned.1.call-done = f32[1024,256]{1,0:T(8,128)} async-done(((f32[4096,256]{1,0:T(8,128)}), f32[1024,256]{1,0:T(8,128)}) %reduce-scatter.2.cloned.1.call-update) | async-done | bytes 1048592 | tf_op jit(solution)/shard_map/reduce_scatter | solution.py:58
  317.0 4.1 fusion.29
  321.1 101.4 %all-reduce.3.cloned.1.call-done = f32[256,256]{1,0:T(8,128)} async-done(((f32[256,256]{1,0:T(8,128)}), f32[256,256]{1,0:T(8,128)}) %all-reduce.3.cloned.1.call-update) | async-done | bytes 262160 | tf_op jit(solution)/shard_map/psum | solution.py:60
  422.5 41.2 %all-reduce.5.cloned.1.call-done = f32[256,256]{1,0:T(8,128)} async-done(((f32[256,256]{1,0:T(8,128)}), f32[256,256]{1,0:T(8,128)}) %all-reduce.5.cloned.1.call-update) | async-done | bytes 262160 | tf_op jit(solution)/shard_map/psum | solution.py:61
  463.8 662.2 %while.33 = (s32[]{:T(128)}, f32[256,256]{1,0:T(8,128)S(1)}, f32[256,256]{1,0:T(8,128)}, s32[]{:T(128)}, s32[]{:T(128)}) while((s32[]{:T(128)}, f32[256,256]{1,0:T(8,128)S(1)}, f32[256,256]{1,0:T(8,128)}, s32[]{:T(128)}, s32[]{:T(128)}) %tuple.80), condition=%wide.region_4.5_spmd.clone.clone, body=%wide.region_3.4_spmd.clone.clone.sunk | while | flops 1902083 | bytes 1063021 | solution.py:22
  464.2 0.7 constant_dynamic-slice_fusion.2
  477.2 0.7 constant_dynamic-slice_fusion.2
  479.8 0.7 constant_dynamic-slice_fusion.2
  482.4 0.7 constant_dynamic-slice_fusion.2
  484.9 0.7 constant_dynamic-slice_fusion.2
  487.5 0.7 constant_dynamic-slice_fusion.2
  490.1 0.7 constant_dynamic-slice_fusion.2
  503.0 0.7 constant_dynamic-slice_fusion.2
  505.6 0.7 constant_dynamic-slice_fusion.2
  508.2 0.7 constant_dynamic-slice_fusion.2
  510.8 0.7 constant_dynamic-slice_fusion.2
  513.4 0.7 constant_dynamic-slice_fusion.2
  526.3 0.7 constant_dynamic-slice_fusion.2
  528.9 0.7 constant_dynamic-slice_fusion.2
  531.5 0.7 constant_dynamic-slice_fusion.2
  534.1 0.7 constant_dynamic-slice_fusion.2
  536.7 0.7 constant_dynamic-slice_fusion.2
  539.3 0.7 constant_dynamic-slice_fusion.2
  552.2 0.7 constant_dynamic-slice_fusion.2
  554.8 0.7 constant_dynamic-slice_fusion.2
  557.4 0.7 constant_dynamic-slice_fusion.2
  560.0 0.7 constant_dynamic-slice_fusion.2
  562.5 0.7 constant_dynamic-slice_fusion.2
  575.5 0.7 constant_dynamic-slice_fusion.2
  578.1 0.7 constant_dynamic-slice_fusion.2
  580.7 0.7 constant_dynamic-slice_fusion.2
  583.2 0.7 constant_dynamic-slice_fusion.2
  585.8 0.7 constant_dynamic-slice_fusion.2
  588.4 0.7 constant_dynamic-slice_fusion.2
  601.3 0.7 constant_dynamic-slice_fusion.2
  603.9 0.7 constant_dynamic-slice_fusion.2
  606.5 0.7 constant_dynamic-slice_fusion.2
  609.1 0.7 constant_dynamic-slice_fusion.2
  611.7 0.7 constant_dynamic-slice_fusion.2
  624.6 0.7 constant_dynamic-slice_fusion.2
  627.2 0.7 constant_dynamic-slice_fusion.2
  629.8 0.7 constant_dynamic-slice_fusion.2
  632.4 0.7 constant_dynamic-slice_fusion.2
  635.0 0.7 constant_dynamic-slice_fusion.2
  637.6 0.7 constant_dynamic-slice_fusion.2
  650.5 0.7 constant_dynamic-slice_fusion.2
  653.1 0.7 constant_dynamic-slice_fusion.2
  655.7 0.7 constant_dynamic-slice_fusion.2
  658.3 0.7 constant_dynamic-slice_fusion.2
  660.8 0.7 constant_dynamic-slice_fusion.2
  673.8 0.7 constant_dynamic-slice_fusion.2
  676.4 0.7 constant_dynamic-slice_fusion.2
  679.0 0.7 constant_dynamic-slice_fusion.2
  1126.7 420.4 %while.32 = (s32[]{:T(128)}, f32[256,256]{1,0:T(8,128)S(1)}, f32[256,256]{1,0:T(8,128)S(1)}, s32[]{:T(128)}, s32[]{:T(128)}, /*index=5*/s32[]{:T(128)}, s32[]{:T(128)}) while((s32[]{:T(128)}, f32[256,256]{1,0:T(8,128)S(1)}, f32[256,256]{1,0:T(8,128)S(1)}, s32[]{:T(128)}, s32[]{:T(128)}, /*index=5*/s32[]{:T(128)}, s32[]{:T(128)}) %tuple.83), condition=%wide.region_6.7_spmd.clone, body=%wide.region_5.6_spmd.clone.sunk | while | flops 984328 | bytes 792242 | solution.py:37
  1547.1 3.2 convolution_multiply_fusion
  (3560 shorter events, 866.2 us)
Async XLA Ops:
  7.2 1.2 copy-start
  7.2 16.4 %copy-start.4 = (s32[176,1]{0,1:T(1,128)S(1)}, s32[176,1]{0,1:T(1,128)}, u32[]{:S(2)}) copy-start(s32[176,1]{0,1:T(1,128)} %param.12) | copy-start | bytes 2116
  7.2 16.4 %copy-start.3 = (s32[176,1]{0,1:T(1,128)S(1)}, s32[176,1]{0,1:T(1,128)}, u32[]{:S(2)}) copy-start(s32[176,1]{0,1:T(1,128)} %param.13) | copy-start | bytes 2116
  13.9 118.2 %all-to-all-start = ((bf16[32,2,256,256]{3,2,1,0:T(8,128)(2,1)}), bf16[32,2,256,256]{3,2,1,0:T(8,128)(2,1)}, u32[]{:S(2)}, u32[]{:S(2)}) async-start(bf16[32,2,256,256]{3,2,1,0:T(8,128)(2,1)} %bitcast.57), calls=%async_computation | async-start | bytes 16777216 | tf_op jit(solution)/shard_map/all_to_all | solution.py:49
  23.6 293.4 %reduce-scatter.2.cloned.1.call-start = ((), (), s32[]{:S(2)}) async-start(), calls=%async_computation.2 | async-start | bytes 5242880 | tf_op jit(solution)/shard_map/reduce_scatter | solution.py:58
  183.5 46.6 %copy-start.2 = (s32[176,1]{0,1:T(1,128)S(1)}, s32[176,1]{0,1:T(1,128)}, u32[]{:S(2)}) copy-start(s32[176,1]{0,1:T(1,128)} %param.11) | copy-start | bytes 2116
  230.1 1320.2 %copy-start.1 = (bf16[8,1,256,256]{3,2,1,0:T(8,128)(2,1)S(1)}, bf16[8,1,256,256]{3,2,1,0:T(8,128)(2,1)}, u32[]{:S(2)}) copy-start(bf16[8,1,256,256]{3,2,1,0:T(8,128)(2,1)} %param.15) | copy-start | bytes 3145732
  254.9 167.6 %all-reduce.3.cloned.1.call-start = ((), (), s32[]{:S(2)}) async-start(), calls=%async_computation.3 | async-start | bytes 524288 | tf_op jit(solution)/shard_map/psum | solution.py:60
  321.1 142.7 %all-reduce.5.cloned.1.call-start = ((), (), s32[]{:S(2)}) async-start(), calls=%async_computation.4 | async-start | bytes 524288 | tf_op jit(solution)/shard_map/psum | solution.py:61
Sparse Core Ops, SparseCore 0:
  255.0 61.9 reduce-scatter.1
  321.2 101.2 all-reduce.2
  424.8 38.9 all-reduce.4
